TPU v7x, 32 devices: a whole 2x2x4 slice. The times are simulated.
32 devices in a mesh: groups: 2 (over x), dp: 16 (over z, y, core).
Axes of the slice: x: 2, y: 2, z: 4, core: 2. Of those that a mesh axis runs over, the one named last changes fastest.
Arguments:
- coords: float32 [3, 8192], P(None, ('groups', 'dp')), parts along dimension 1, may hold values from -1 to 1
- forcing: float32 [3, 8192], P(None, ('groups', 'dp')), parts along dimension 1, may hold values from -6 to 6
- bins: int32 [8192], P(('groups', 'dp')), parts along dimension 0, may hold values from 0 to 15
- counts: int32 [32], P(('groups', 'dp')), parts along dimension 0, may hold values from 1 to 255, as said below
- bin_weight: float32 [32], P('groups'), parts along dimension 0, may hold values from 0.3 to 3
- w_in: float32 [6, 1024], P('groups'), parts along dimension 0, may hold values from -6 to 6
- b_in: float32 [2048], P('groups'), parts along dimension 0, may hold values from -3 to 3
- w_mid: bfloat16 [2048, 1024], P('groups'), parts along dimension 0, may hold values from -0.1875 to 0.1875
- b_mid: float32 [2048], P('groups'), parts along dimension 0, may hold values from -2 to 2
- w_out: bfloat16 [2048, 4], P('groups'), parts along dimension 0, may hold values from -0.1875 to 0.1875
- b_out: float32 [8], P('groups'), parts along dimension 0, may hold values from -3 to 3
Outputs:
- update: float32 [2048, 4], P(('groups', 'dp')), parts along dimension 0
- inverse_factor: float32 [2048, 1024], P(('groups', 'dp')), parts along dimension 0
There are 2 independent parts, one for each index of `groups`. A program takes and returns all parts, laid end to end along the dimension named above; each array names one. Nothing has to cross between parts.
Inputs may be any that keep to these rules, and one draw needn't show every extreme that they name: Each dp device has 256 slots of points; the first counts[i] of device i are live. The live points of a device and of the device half the dp axis away number at most 256 together, exactly 256 for some pair.
All inputs are finite; a program needn't handle non-finite values. Where the computation divides by a largest or mean magnitude, that divisor is 1e-20 or more.
Results may differ from a plain program's by a relative error of at most 0.0034.
Values sent between devices are 32-bit elements; how exact they have to be, the bound alone decides.
A program may use at most 64 MiB of HBM per device.

v0:
```python
import jax
import jax.numpy as jnp
from jax import lax
from jax.sharding import PartitionSpec as P

ITERS = 6


VISCOSITY = 0.05
DAMP_FACTOR = 1.0
DAMP_OUTPUT = 0.1


def point_weights(bin_row, count, bin_weight, slots):
    levels = jnp.arange(bin_weight.shape[0], dtype=jnp.int32)
    lookup = jnp.sum(
        jnp.where(bin_row[None, :] == levels[:, None], bin_weight[:, None], jnp.float32(0.0)), 0
    )
    live = jnp.arange(slots, dtype=jnp.int32) < count
    return jnp.where(live, lookup, jnp.float32(0.0))


def taylor(points, w_in, b_in, w_mid, b_mid):
    width = w_mid.shape[0]
    pre = (
        points[0][:, None] * w_in[0]
        + points[1][:, None] * w_in[1]
        + points[2][:, None] * w_in[2]
        + b_in
    )
    act = jnp.tanh(pre)
    slope = 1.0 - act * act
    curve_in = jnp.sum(w_in * w_in, 0)
    first = jnp.stack(
        [act, slope * w_in[0], slope * w_in[1], slope * w_in[2], -2.0 * act * slope * curve_in]
    ).astype(jnp.bfloat16)
    count = points.shape[1]
    mixed = jnp.dot(
        first.reshape(5 * count, width), w_mid, preferred_element_type=jnp.float32
    ).reshape(5, count, width)
    act_two = jnp.tanh(mixed[0] + b_mid)
    slope_two = 1.0 - act_two * act_two
    grads = mixed[1:4]
    lap_two = slope_two * mixed[4] - 2.0 * act_two * slope_two * jnp.sum(grads * grads, 0)
    return jnp.concatenate([act_two[None], slope_two[None] * grads, lap_two[None]], 0).astype(
        jnp.bfloat16
    )


def residual_loss(heads, points, pushes, weights):
    value = heads[0]
    slopes = heads[1:4]
    curve = heads[4]
    height = points[1]
    wall = 1.0 - height * height
    flat_zero = jnp.zeros_like(height)
    wall_slope = jnp.stack([flat_zero, -2.0 * height, flat_zero])
    vel = wall[:, None] * value[:, :3]
    vel_slope = wall_slope[:, :, None] * value[None, :, :3] + wall[None, :, None] * slopes[:, :, :3]
    vel_lap = (
        -2.0 * value[:, :3]
        + 2.0 * jnp.sum(wall_slope[:, :, None] * slopes[:, :, :3], 0)
        + wall[:, None] * curve[:, :3]
    )
    convect = jnp.sum(vel.T[:, :, None] * vel_slope, 0)
    momentum = convect + slopes[:, :, 3].T - VISCOSITY * vel_lap - pushes.T
    divergence = vel_slope[0, :, 0] + vel_slope[1, :, 1] + vel_slope[2, :, 2]
    return 0.5 * jnp.sum(weights * (jnp.sum(momentum * momentum, 1) + divergence * divergence))


def on_device(coords, forcing, bins, counts, bin_weight, w_in, b_in, w_mid, b_mid, w_out, b_out):
    slots = coords.shape[1]
    width = w_mid.shape[0]
    own_weights = point_weights(bins, counts[0], bin_weight, slots)
    count = coords.shape[1]
    jets = taylor(coords, w_in, b_in, w_mid, b_mid)
    flat = jets.reshape(5 * count, width)
    heads = jnp.dot(flat, w_out, preferred_element_type=jnp.float32).reshape(5, count, 4)
    heads = heads.at[0].add(b_out)
    cotangent = jax.grad(residual_loss)(heads, coords, forcing, own_weights).reshape(5 * count, 4)
    grad_part = lax.dot_general(
        flat,
        cotangent.astype(jnp.bfloat16),
        (((0,), (0,)), ((), ())),
        preferred_element_type=jnp.float32,
    )
    outer = lax.dot_general(
        cotangent,
        cotangent,
        (((0,), (0,)), ((), ())),
        precision=lax.Precision.HIGHEST,
        preferred_element_type=jnp.float32,
    )
    grad_sum, outer_sum, weight_sum = lax.psum((grad_part, outer, jnp.sum(own_weights)), "dp")
    scaled = (jets * own_weights[None, :, None]).astype(jnp.bfloat16).reshape(5 * count, width)
    rows = width // lax.axis_size("dp")
    gram_part = lax.psum_scatter(
        lax.dot_general(scaled, flat, (((0,), (0,)), ((), ())), preferred_element_type=jnp.float32),
        "dp",
        scatter_dimension=0,
        tiled=True,
    )
    row_ids = lax.axis_index("dp") * rows + jnp.arange(rows, dtype=jnp.int32)
    ident = (row_ids[:, None] == jnp.arange(width, dtype=jnp.int32)[None, :]).astype(jnp.float32)
    factor = gram_part / weight_sum + DAMP_FACTOR * ident
    bound = lax.pmax(jnp.max(jnp.sum(jnp.abs(factor), 1)), "dp")
    iterate = 2.0 / bound * ident - factor / (bound * bound)
    for step in range(ITERS - 1):
        whole = lax.all_gather(iterate, "dp", axis=0, tiled=True)
        mine = lax.dynamic_slice_in_dim(whole, lax.axis_index("dp") * rows, rows, 0)
        product = jnp.dot(
            factor, whole, precision=lax.Precision.HIGHEST, preferred_element_type=jnp.float32
        )
        iterate = 2.0 * mine - jnp.dot(
            product, whole, precision=lax.Precision.HIGHEST, preferred_element_type=jnp.float32
        )
    output_factor = 4.0 * outer_sum / jnp.trace(outer_sum) + DAMP_OUTPUT * jnp.eye(
        4, dtype=jnp.float32
    )
    merged = jnp.dot(
        iterate,
        grad_sum / weight_sum,
        precision=lax.Precision.HIGHEST,
        preferred_element_type=jnp.float32,
    )
    lower = jnp.linalg.cholesky(output_factor)
    update = jax.scipy.linalg.cho_solve((lower, True), merged.T).T
    return (update, iterate)


def solution(mesh):
    placed = (
        P(None, ("groups", "dp")),
        P(None, ("groups", "dp")),
        P(("groups", "dp")),
        P(("groups", "dp")),
        P("groups"),
        P("groups", None),
        P("groups"),
        P("groups", None),
        P("groups"),
        P("groups", None),
        P("groups"),
    )
    return jax.shard_map(
        on_device,
        mesh=mesh,
        in_specs=placed,
        out_specs=(P(("groups", "dp"), None), P(("groups", "dp"), None)),
        check_vma=False,
    )
```

profile of v0, /device:TPU:0, one launch (start us, length us, event | category | flops | bytes accessed | tf_op | source)
XLA Modules:
  0.0 443.5 jit_solution(15831619859593136285)
XLA Ops:
  7.2 0.9 fusion.47
  8.1 0.7 multiply_reduce_fusion.1
  8.9 0.8 broadcast_multiply_fusion.3
  9.7 1.0 fusion.12
  10.7 1.1 fusion.9
  11.8 1.1 fusion.10
  13.0 1.1 fusion.11
  14.1 1.2 fusion.8
  15.4 2.9 fusion.49
  18.3 0.4 slice.133
  18.7 0.4 multiply_reduce_fusion
  19.4 0.5 fusion.13
  19.9 0.6 multiply_convert_fusion.2
  21.2 0.4 copy-done.7
  21.6 5.0 %fusion.2 = f32[1024,1024]{1,0:T(8,128)} fusion(f32[256]{0:T(256)S(1)} %get-tuple-element.49, bf16[1,256,1024]{2,1,0:T(8,128)(2,1)S(1)} %get-tuple-element.27, bf16[3,256,1024]{2,1,0:T(8,128)(2,1)S(1)} %multiply_convert_fusion.2, bf16[1,256,1024]{2,1,0:T(8,128)(2,1)S(1)} %get-tuple-element.25), kind=kOutput, calls=%fused_computation.6 | convolution fusion | flops 2693529600 | bytes 6816768 | tf_op jit(solution)/shard_map/dot_general | solution.py:98
  26.7 0.6 copy-done.15
  27.3 2.3 fusion.21
  30.1 1.7 convolution_bitcast_fusion
  31.9 0.6 reduce_sum.110
  32.5 72.6 %all-reduce.13 = (f32[]{:T(128)}, f32[1024,4]{1,0:T(8,128)S(1)}, f32[4,4]{0,1:T(4,128)S(1)}) all-reduce(f32[]{:T(128)} %reduce_sum.110, f32[1024,4]{1,0:T(8,128)} %convolution_bitcast_fusion, f32[4,4]{0,1:T(4,128)S(1)} %convolution_bitcast_fusion.1), channel_id=1, replica_groups=mesh['groups'=2,'dp'=16] {'dp'}, use_global_device_ids=true, to_apply=%region_13.14 | all-reduce | flops 4113 | bytes 32904 | tf_op jit(solution)/shard_map/psum | solution.py:94
  105.1 0.9 reduce-scatter.2.cloned.1.call-done
  106.0 1.8 abs_reduce_fusion
  107.8 0.6 reduce_max.9
  108.5 30.7 %pmax.7 = f32[]{:T(128)} all-reduce(f32[]{:T(128)} %reduce_max.9), channel_id=1, replica_groups=mesh['groups'=2,'dp'=16] {'dp'}, use_global_device_ids=true, to_apply=%region_17.18 | all-reduce | flops 1 | bytes 8 | tf_op jit(solution)/shard_map/pmax | solution.py:106
  141.1 2.4 divide_subtract_fusion
  143.8 47.7 %all-gather.6.cloned.1.call-done = f32[1024,1024]{1,0:T(8,128)} async-done(((f32[64,1024]{1,0:T(8,128)}), f32[1024,1024]{1,0:T(8,128)}) %all-gather.6.cloned.1.call-update) | async-done | bytes 4194320 | tf_op jit(solution)/shard_map/all_gather | solution.py:109
  191.5 5.9 %fusion.45 = f32[64,1024]{1,0:T(8,128)S(1)} fusion(f32[1024,1024]{1,0:T(8,128)} %all-gather.6.cloned.1.call-done, f32[64,1024]{1,0:T(8,128)} %reduce-scatter.2.cloned.1.call-done, f32[]{:T(128)} %get-tuple-element.16, s32[64]{0:T(128)S(1)} %iota_add_fusion), kind=kOutput, calls=%fused_computation.110 | convolution fusion | flops 805568512 | bytes 4718852 | tf_op jit(solution)/shard_map/dot_general | solution.py:111
  197.5 3.4 convolution_subtract_fusion.4
  200.9 49.2 %all-gather.8.cloned.1.call-done = f32[1024,1024]{1,0:T(8,128)} async-done(((f32[64,1024]{1,0:T(8,128)}), f32[1024,1024]{1,0:T(8,128)}) %all-gather.8.cloned.1.call-update) | async-done | bytes 4194320 | tf_op jit(solution)/shard_map/all_gather | solution.py:109
  250.1 5.8 %fusion.44 = f32[64,1024]{1,0:T(8,128)S(1)} fusion(f32[1024,1024]{1,0:T(8,128)} %all-gather.8.cloned.1.call-done, f32[64,1024]{1,0:T(8,128)S(1)} %copy-done.6, f32[]{:T(128)} %get-tuple-element.16, s32[64]{0:T(128)S(1)} %iota_add_fusion), kind=kOutput, calls=%fused_computation.109 | convolution fusion | flops 805568512 | bytes 4718852 | tf_op jit(solution)/shard_map/dot_general | solution.py:111
  255.9 3.4 convolution_subtract_fusion.3
  259.3 49.2 %all-gather.10.cloned.1.call-done = f32[1024,1024]{1,0:T(8,128)} async-done(((f32[64,1024]{1,0:T(8,128)}), f32[1024,1024]{1,0:T(8,128)}) %all-gather.10.cloned.1.call-update) | async-done | bytes 4194320 | tf_op jit(solution)/shard_map/all_gather | solution.py:109
  308.5 5.8 %fusion.43 = f32[64,1024]{1,0:T(8,128)S(1)} fusion(f32[1024,1024]{1,0:T(8,128)} %all-gather.10.cloned.1.call-done, f32[64,1024]{1,0:T(8,128)S(1)} %copy-done.6, f32[]{:T(128)} %get-tuple-element.16, s32[64]{0:T(128)S(1)} %iota_add_fusion), kind=kOutput, calls=%fused_computation.108 | convolution fusion | flops 805568512 | bytes 4718852 | tf_op jit(solution)/shard_map/dot_general | solution.py:111
  314.3 3.4 convolution_subtract_fusion.2
  318.0 49.1 %all-gather.12.cloned.1.call-done = f32[1024,1024]{1,0:T(8,128)} async-done(((f32[64,1024]{1,0:T(8,128)}), f32[1024,1024]{1,0:T(8,128)}) %all-gather.12.cloned.1.call-update) | async-done | bytes 4194320 | tf_op jit(solution)/shard_map/all_gather | solution.py:109
  367.1 5.8 %fusion.42 = f32[64,1024]{1,0:T(8,128)S(1)} fusion(f32[1024,1024]{1,0:T(8,128)} %all-gather.12.cloned.1.call-done, f32[64,1024]{1,0:T(8,128)S(1)} %copy-done.6, f32[]{:T(128)} %get-tuple-element.16, s32[64]{0:T(128)S(1)} %iota_add_fusion), kind=kOutput, calls=%fused_computation.107 | convolution fusion | flops 805568512 | bytes 4718852 | tf_op jit(solution)/shard_map/dot_general | solution.py:111
  372.9 3.4 convolution_subtract_fusion.1
  376.3 0.6 select_reduce_fusion.2
  376.9 0.6 divide_add_fusion
  377.6 0.6 fusion.36
  378.3 0.4 cholesky.17
  378.8 0.7 compare_reduce_fusion
  379.5 0.6 select_select_fusion
  380.6 45.0 %all-gather.14.cloned.1.call-done = f32[1024,1024]{1,0:T(8,128)} async-done(((f32[64,1024]{1,0:T(8,128)}), f32[1024,1024]{1,0:T(8,128)}) %all-gather.14.cloned.1.call-update) | async-done | bytes 4194320 | tf_op jit(solution)/shard_map/all_gather | solution.py:109
  425.6 5.8 %fusion.41 = f32[64,1024]{1,0:T(8,128)S(1)} fusion(f32[1024,1024]{1,0:T(8,128)} %all-gather.14.cloned.1.call-done, f32[64,1024]{1,0:T(8,128)S(1)} %copy-done.6, f32[]{:T(128)} %get-tuple-element.16, s32[64]{0:T(128)S(1)} %iota_add_fusion), kind=kOutput, calls=%fused_computation.106 | convolution fusion | flops 805568512 | bytes 4718852 | tf_op jit(solution)/shard_map/dot_general | solution.py:111
  431.4 2.7 convolution_subtract_fusion
  434.1 1.6 fusion.14
  435.9 0.7 fusion.32
  (70 shorter events, 2.6 us)
Async XLA Ops:
  7.2 8.2 %copy-start = (bf16[1024,1024]{1,0:T(8,128)(2,1)S(1)}, bf16[1024,1024]{1,0:T(8,128)(2,1)}, u32[]{:S(2)}) copy-start(bf16[1024,1024]{1,0:T(8,128)(2,1)} %param.20) | copy-start | bytes 6291460
  7.2 98.8 %reduce-scatter.2.cloned.1.call-start = ((), (), s32[]{:S(2)}) async-start(), calls=%async_computation.1 | async-start | bytes 4456448 | tf_op jit(solution)/shard_map/reduce_scatter | solution.py:97
  18.7 0.7 copy-start.11
  19.8 1.2 copy-start.12
  19.9 1.2 copy-start.13
  20.4 1.2 copy-start.7
  26.6 0.7 copy-start.15
  26.6 3.0 copy-start.14
  26.6 3.2 copy-start.10
  26.6 164.9 %all-gather.6.cloned.1.call-start = ((), (), s32[]{:S(2)}) async-start(), calls=%async_computation.2 | async-start | bytes 4456448 | tf_op jit(solution)/shard_map/all_gather | solution.py:109
  27.3 2.8 copy-start.8
  143.6 106.5 %all-gather.8.cloned.1.call-start = ((), (), s32[]{:S(2)}) async-start(), calls=%async_computation.3 | async-start | bytes 4456448 | tf_op jit(solution)/shard_map/all_gather | solution.py:109
  191.5 5.9 %copy-start.2 = (f32[1024,1024]{1,0:T(8,128)S(1)}, f32[1024,1024]{1,0:T(8,128)}, u32[]{:S(2)}) copy-start(f32[1024,1024]{1,0:T(8,128)} %all-gather.6.cloned.1.call-done) | copy-start | bytes 12582916
  197.4 52.6 %copy-start.6 = (f32[64,1024]{1,0:T(8,128)S(1)}, f32[64,1024]{1,0:T(8,128)}, u32[]{:S(2)}) copy-start(f32[64,1024]{1,0:T(8,128)} %reduce-scatter.2.cloned.1.call-done) | copy-start | bytes 786436
  200.8 107.6 %all-gather.10.cloned.1.call-start = ((), (), s32[]{:S(2)}) async-start(), calls=%async_computation.4 | async-start | bytes 4456448 | tf_op jit(solution)/shard_map/all_gather | solution.py:109
  250.1 5.8 %copy-start.3 = (f32[1024,1024]{1,0:T(8,128)S(1)}, f32[1024,1024]{1,0:T(8,128)}, u32[]{:S(2)}) copy-start(f32[1024,1024]{1,0:T(8,128)} %all-gather.8.cloned.1.call-done) | copy-start | bytes 12582916
  259.3 107.8 %all-gather.12.cloned.1.call-start = ((), (), s32[]{:S(2)}) async-start(), calls=%async_computation.5 | async-start | bytes 4456448 | tf_op jit(solution)/shard_map/all_gather | solution.py:109
  308.5 5.8 %copy-start.4 = (f32[1024,1024]{1,0:T(8,128)S(1)}, f32[1024,1024]{1,0:T(8,128)}, u32[]{:S(2)}) copy-start(f32[1024,1024]{1,0:T(8,128)} %all-gather.10.cloned.1.call-done) | copy-start | bytes 12582916
  317.7 107.9 %all-gather.14.cloned.1.call-start = ((), (), s32[]{:S(2)}) async-start(), calls=%async_computation.6 | async-start | bytes 4456448 | tf_op jit(solution)/shard_map/all_gather | solution.py:109
  367.1 5.8 %copy-start.5 = (f32[1024,1024]{1,0:T(8,128)S(1)}, f32[1024,1024]{1,0:T(8,128)}, u32[]{:S(2)}) copy-start(f32[1024,1024]{1,0:T(8,128)} %all-gather.12.cloned.1.call-done) | copy-start | bytes 12582916
  425.6 5.8 %copy-start.1 = (f32[1024,1024]{1,0:T(8,128)S(1)}, f32[1024,1024]{1,0:T(8,128)}, u32[]{:S(2)}) copy-start(f32[1024,1024]{1,0:T(8,128)} %all-gather.14.cloned.1.call-done) | copy-start | bytes 12582916
  434.1 2.6 copy-start.9
Sparse Core Ops, SparseCore 0:
  26.7 79.2 reduce-scatter.1
  143.7 47.7 all-gather.5
  201.0 49.0 all-gather.7
  259.4 49.0 all-gather.9
  317.8 49.1 all-gather.11
  376.4 49.0 all-gather.13
where the time goes:
time: 444 us; the launch traced here: 443 us
  waiting for transfers between devices  241 us (54%)
  blocking collectives  103 us (23%)
  matrix products  59.9 us (13%)
  other arithmetic  18.3 us (4%)
  between operations  17.1 us (4%)
    all_gather x5, waiting for transfers between devices, on_device(): whole = lax.all_gather(iterate, 'dp', axis=0, tiled=True)  240 us
    psum x1, blocking collectives, on_device(): lax.psum((grad_part, outer, jnp.sum(own_weights)), 'dp')  72.6 us
    pmax x1, blocking collectives, on_device(): bound = lax.pmax(jnp.max(jnp.sum(jnp.abs(factor), 1)), 'dp')  30.7 us
    dot_general x5, matrix products, on_device(): jnp.dot(factor, whole, precision=lax.Precision.HIGHEST, preferred_element...  29.2 us
    dot_general x5, matrix products, on_device(): jnp.dot(product, whole, precision=lax.Precision.HIGHEST, preferred_elemen...  16.1 us
  transfers between devices with their start and end apart: 6, of which 6 were waited for; matrix products, arithmetic and copies ran while one was open for 2% of the time, Pallas kernels for 0%

commit v1 on v0

v1 whole, which is shorter than its diff:
```python
import functools

import jax
import jax.numpy as jnp
from jax import lax
from jax.experimental import pallas as pl
from jax.experimental.pallas import tpu as pltpu
from jax.sharding import PartitionSpec as P

ITERS = 6
VISCOSITY = 0.05
DAMP_FACTOR = 1.0
DAMP_OUTPUT = 0.1

TILE = 256
MESH = pl.DeviceIdType.MESH
VMEM = pl.BlockSpec(memory_space=pltpu.VMEM)
BIG = 56 * 1024 * 1024
ROWS_DOT = (((1,), (1,)), ((), ()))
F32 = jnp.float32
BF16 = jnp.bfloat16


def packed_points(coords, forcing, bins, count, bin_weight, upper):
    slots = coords.shape[1]
    levels = jnp.arange(bin_weight.shape[0], dtype=jnp.int32)
    lookup = jnp.sum(jnp.where(bins[None, :] == levels[:, None], bin_weight[:, None], F32(0.0)), 0)
    every = jnp.concatenate([coords, forcing, lookup[None], jnp.zeros((1, slots), F32)], 0)
    live = jnp.arange(slots, dtype=jnp.int32) < count
    every = jnp.where(live[None, :], every, F32(0.0))
    return jnp.where(upper, every[:, ::-1], every)


def share_points(axis_size, own_ref, out_ref, held, send_sem, recv_sem):
    half = axis_size // 2
    me = lax.axis_index("dp")
    place = me // 2
    parity = me % 2
    barrier = pltpu.get_barrier_semaphore()
    for hop in range(1, half):
        other = (place + hop) % half
        pl.semaphore_signal(
            barrier, inc=1, device_id={"dp": other * 2 + parity}, device_id_type=MESH
        )
    pl.semaphore_wait(barrier, half - 1)
    copies = []
    for hop in range(1, half):
        other = (place + hop) % half
        copy = pltpu.make_async_remote_copy(
            src_ref=own_ref,
            dst_ref=held.at[place],
            send_sem=send_sem.at[hop],
            recv_sem=recv_sem.at[place],
            device_id={"dp": other * 2 + parity},
            device_id_type=MESH,
        )
        copy.start()
        copies.append(copy)
    held[place] = own_ref[...]
    for hop in range(1, half):
        source = (place + hop) % half
        pltpu.make_async_remote_copy(
            src_ref=own_ref,
            dst_ref=held.at[source],
            send_sem=send_sem.at[hop],
            recv_sem=recv_sem.at[source],
            device_id={"dp": source * 2 + parity},
            device_id_type=MESH,
        ).wait_recv()
    for pair in range(half // 2):
        out_ref[pair] = held[pair] + held[pair + half // 2]
    for copy in copies:
        copy.wait_send()


def point_loss(heads, height, pushes, weight):
    value, slopes, curve = heads[0], heads[1:4], heads[4]
    wall = 1.0 - height * height
    wall_slope = -2.0 * height
    vel = [wall * value[i] for i in range(3)]
    vel_slope = [[wall * slopes[k][i] for i in range(3)] for k in range(3)]
    for i in range(3):
        vel_slope[1][i] = wall_slope * value[i] + vel_slope[1][i]
    total = vel_slope[0][0] + vel_slope[1][1] + vel_slope[2][2]
    total = total * total
    for i in range(3):
        lap = -2.0 * value[i] + 2.0 * (wall_slope * slopes[1][i]) + wall * curve[i]
        convect = vel[0] * vel_slope[0][i] + vel[1] * vel_slope[1][i] + vel[2] * vel_slope[2][i]
        momentum = convect + slopes[i][3] - VISCOSITY * lap - pushes[i]
        total = total + momentum * momentum
    return 0.5 * (weight * total)


def point_terms(points_ref, cols_ref, mid_ref, out_ref, bias_ref, gram_ref, small_ref, first, jets, scaled):
    width = mid_ref.shape[0]
    slots = points_ref.shape[2]
    tiles = width // TILE
    step = pl.program_id(0)

    @pl.when(step == 0)
    def _():
        gram_ref[...] = jnp.zeros_like(gram_ref)
        small_ref[...] = jnp.zeros_like(small_ref)

    row = [points_ref[0, k : k + 1, :] for k in range(7)]
    weight = row[6]

    def column(part, k):
        return cols_ref[part * TILE : (part + 1) * TILE, k : k + 1]

    for part in range(tiles):
        rows = pl.ds(part * TILE, TILE)
        w = [column(part, k) for k in range(3)]
        pre = row[0] * w[0] + row[1] * w[1] + row[2] * w[2] + column(part, 3)
        act = jnp.tanh(pre)
        slope = 1.0 - act * act
        curve_in = w[0] * w[0] + w[1] * w[1] + w[2] * w[2]
        first[rows, 0:slots] = act.astype(BF16)
        for k in range(3):
            first[rows, (k + 1) * slots : (k + 2) * slots] = (slope * w[k]).astype(BF16)
        first[rows, 4 * slots : 5 * slots] = (-2.0 * act * slope * curve_in).astype(BF16)
    for part in range(tiles):
        rows = pl.ds(part * TILE, TILE)
        mixed = jnp.dot(mid_ref[rows, :], first[...], preferred_element_type=F32)
        mixed = [mixed[:, k * slots : (k + 1) * slots] for k in range(5)]
        act = jnp.tanh(mixed[0] + column(part, 4))
        slope = 1.0 - act * act
        squares = mixed[1] * mixed[1] + mixed[2] * mixed[2] + mixed[3] * mixed[3]
        jet = [act, slope * mixed[1], slope * mixed[2], slope * mixed[3]]
        jet.append(slope * mixed[4] - 2.0 * act * slope * squares)
        for k in range(5):
            half = jet[k].astype(BF16)
            jets[rows, k * slots : (k + 1) * slots] = half
            scaled[rows, k * slots : (k + 1) * slots] = (half.astype(F32) * weight).astype(BF16)
    block = 0
    for i in range(tiles):
        rows = pl.ds(i * TILE, TILE)
        part = lax.dot_general(
            scaled[rows, :], jets[i * TILE :, :], ROWS_DOT, preferred_element_type=F32
        )
        for j in range(tiles - i):
            gram_ref[block] += part[:, j * TILE : (j + 1) * TILE]
            block += 1
    heads = jnp.dot(out_ref[...], jets[...], preferred_element_type=F32)
    table = [[heads[i : i + 1, k * slots : (k + 1) * slots] for i in range(4)] for k in range(5)]
    table[0] = [table[0][i] + bias_ref[i : i + 1, 0:1] for i in range(4)]
    _, pull = jax.vjp(lambda t: point_loss(t, row[1], row[3:6], weight), table)
    (slant,) = pull(jnp.ones_like(weight))
    at = lax.broadcasted_iota(jnp.int32, (8, slots), 0)
    pieces = []
    for k in range(5):
        piece = jnp.zeros((8, slots), F32)
        for i in range(4):
            piece = jnp.where(at == i, slant[k][i], piece)
        if k == 0:
            piece = jnp.where(at == 4, weight, piece)
            piece = jnp.where(at == 5, F32(1.0), piece)
        pieces.append(piece)
    cot = jnp.concatenate(pieces, 1)
    small_ref[0:8, :] += lax.dot_general(
        cot.astype(BF16), jets[...], ROWS_DOT, preferred_element_type=F32
    )
    small_ref[8:16, 0:8] += lax.dot_general(
        cot, cot, ROWS_DOT, precision=lax.Precision.HIGHEST, preferred_element_type=F32
    )


def swap_sums(gram_ref, small_ref, gram_out, small_out, send_sem, recv_sem):
    other = lax.axis_index("dp")
    other = other + 1 - 2 * (other % 2)
    barrier = pltpu.get_barrier_semaphore()
    pl.semaphore_signal(barrier, inc=1, device_id={"dp": other}, device_id_type=MESH)
    pl.semaphore_wait(barrier, 1)
    copies = []
    for at, (source, target) in enumerate(((gram_ref, gram_out), (small_ref, small_out))):
        copy = pltpu.make_async_remote_copy(
            src_ref=source,
            dst_ref=target,
            send_sem=send_sem.at[at],
            recv_sem=recv_sem.at[at],
            device_id={"dp": other},
            device_id_type=MESH,
        )
        copy.start()
        copies.append(copy)
    for copy in copies:
        copy.wait()


def solve_rows(own_rows, gram_a, gram_b, small_a, small_b, inverse_ref, update_ref, full, high, low):
    width = full.shape[0]
    tiles = width // TILE
    first_row = pl.multiple_of(lax.axis_index("dp") * own_rows, own_rows)
    small = small_a[...] + small_b[...]
    weight_sum = small[12:13, 5:6]
    block = 0
    largest = jnp.zeros((1, 1), F32)
    for i in range(tiles):
        for j in range(i, tiles):
            piece = (gram_a[block] + gram_b[block]) / weight_sum
            block += 1
            if i == j:
                here = lax.broadcasted_iota(jnp.int32, (TILE, TILE), 0)
                there = lax.broadcasted_iota(jnp.int32, (TILE, TILE), 1)
                piece = piece + jnp.where(here == there, F32(DAMP_FACTOR), F32(0.0))
            full[i * TILE : (i + 1) * TILE, j * TILE : (j + 1) * TILE] = piece
            if i != j:
                full[j * TILE : (j + 1) * TILE, i * TILE : (i + 1) * TILE] = piece.T
    for i in range(tiles):
        sums = jnp.sum(jnp.abs(full[i * TILE : (i + 1) * TILE, :]), 1, keepdims=True)
        largest = jnp.maximum(largest, jnp.max(sums, 0, keepdims=True))
    shrink = 1.0 / largest

    def put(at, rows, value):
        full[rows, :] = value
        upper = value.astype(BF16)
        high[at, rows, :] = upper
        low[rows, :] = (value - upper.astype(F32)).astype(BF16)

    for i in range(tiles):
        rows = pl.ds(i * TILE, TILE)
        put(0, rows, full[rows, :] * shrink)
    mine = full[pl.ds(first_row, own_rows), :]
    at_row = lax.broadcasted_iota(jnp.int32, mine.shape, 0) + first_row
    at_col = lax.broadcasted_iota(jnp.int32, mine.shape, 1)
    iterate = jnp.where(at_row == at_col, F32(2.0), F32(0.0)) - mine

    def times(value, at):
        upper = value.astype(BF16)
        lower = (value - upper.astype(F32)).astype(BF16)
        both = jnp.dot(jnp.concatenate([upper, lower], 0), high[at], preferred_element_type=F32)
        rest = jnp.dot(upper, low[...], preferred_element_type=F32)
        return both[:own_rows] + (both[own_rows:] + rest)

    at = 0
    for _ in range(ITERS - 2):
        for i in range(tiles):
            rows = pl.ds(i * TILE, TILE)
            square = jnp.dot(high[at, rows, :], high[at], preferred_element_type=F32)
            put(1 - at, rows, 2.0 * full[rows, :] - square)
        at = 1 - at
        iterate = 2.0 * iterate - times(iterate, at)
    turned = iterate - times(iterate, at)
    turned = turned - times(turned, at)
    iterate = (iterate + turned) * shrink
    inverse_ref[...] = iterate
    merged = lax.dot_general(
        small[0:8, :] / weight_sum,
        iterate,
        ROWS_DOT,
        precision=lax.Precision.HIGHEST,
        preferred_element_type=F32,
    )
    outer = [[small[8 + i : 9 + i, j : j + 1] for j in range(4)] for i in range(4)]
    trace = outer[0][0] + outer[1][1] + outer[2][2] + outer[3][3]
    lower = [[None] * 4 for _ in range(4)]
    for i in range(4):
        for j in range(i + 1):
            entry = 4.0 * outer[i][j] / trace
            if i == j:
                entry = entry + DAMP_OUTPUT
            for k in range(j):
                entry = entry - lower[i][k] * lower[j][k]
            lower[i][j] = jnp.sqrt(entry) if i == j else entry / lower[j][j]
    solved = [merged[i : i + 1, :] for i in range(4)]
    for i in range(4):
        for k in range(i):
            solved[i] = solved[i] - lower[i][k] * solved[k]
        solved[i] = solved[i] / lower[i][i]
    for i in reversed(range(4)):
        for k in range(i + 1, 4):
            solved[i] = solved[i] - lower[k][i] * solved[k]
        solved[i] = solved[i] / lower[i][i]
    at = lax.broadcasted_iota(jnp.int32, (8, own_rows), 0)
    update = jnp.zeros((8, own_rows), F32)
    for i in range(4):
        update = jnp.where(at == i, solved[i], update)
    update_ref[...] = update


def on_device(coords, forcing, bins, counts, bin_weight, w_in, b_in, w_mid, b_mid, w_out, b_out):
    slots = coords.shape[1]
    width = w_mid.shape[0]
    size = lax.axis_size("dp")
    half = size // 2
    pairs = half // 2
    tiles = width // TILE
    blocks = tiles * (tiles + 1) // 2
    own_rows = width // size
    upper = lax.axis_index("dp") >= half
    own = packed_points(coords, forcing, bins, counts[0], bin_weight, upper)
    points = pl.pallas_call(
        functools.partial(share_points, size),
        out_shape=jax.ShapeDtypeStruct((pairs, 8, slots), F32),
        in_specs=[VMEM],
        out_specs=VMEM,
        scratch_shapes=[
            pltpu.VMEM((half, 8, slots), F32),
            pltpu.SemaphoreType.DMA((half,)),
            pltpu.SemaphoreType.DMA((half,)),
        ],
        compiler_params=pltpu.CompilerParams(collective_id=0, has_side_effects=True),
        name="share_points",
    )(own)
    cols = jnp.concatenate([w_in, b_in[None], b_mid[None], jnp.zeros((3, width), F32)], 0).T
    out_rows = jnp.concatenate([w_out.T, jnp.zeros((12, width), BF16)], 0)
    bias = jnp.concatenate([b_out, jnp.zeros((4,), F32)])[:, None]
    fixed = lambda *shape: pl.BlockSpec(shape, lambda i: (0,) * len(shape))
    gram, small = pl.pallas_call(
        point_terms,
        grid=(pairs,),
        out_shape=(
            jax.ShapeDtypeStruct((blocks, TILE, TILE), F32),
            jax.ShapeDtypeStruct((16, width), F32),
        ),
        in_specs=[
            pl.BlockSpec((1, 8, slots), lambda i: (i, 0, 0)),
            fixed(width, 8),
            fixed(width, width),
            fixed(16, width),
            fixed(8, 1),
        ],
        out_specs=(fixed(blocks, TILE, TILE), fixed(16, width)),
        scratch_shapes=[pltpu.VMEM((width, 5 * slots), BF16) for _ in range(3)],
        compiler_params=pltpu.CompilerParams(vmem_limit_bytes=BIG),
        name="point_terms",
    )(points, cols, w_mid.T, out_rows, bias)
    gram_other, small_other = pl.pallas_call(
        swap_sums,
        out_shape=(
            jax.ShapeDtypeStruct(gram.shape, F32),
            jax.ShapeDtypeStruct(small.shape, F32),
        ),
        in_specs=[VMEM, VMEM],
        out_specs=(VMEM, VMEM),
        scratch_shapes=[pltpu.SemaphoreType.DMA((2,)), pltpu.SemaphoreType.DMA((2,))],
        compiler_params=pltpu.CompilerParams(
            collective_id=1, has_side_effects=True, vmem_limit_bytes=BIG
        ),
        name="swap_sums",
    )(gram, small)
    inverse, update = pl.pallas_call(
        functools.partial(solve_rows, own_rows),
        out_shape=(
            jax.ShapeDtypeStruct((own_rows, width), F32),
            jax.ShapeDtypeStruct((8, own_rows), F32),
        ),
        in_specs=[VMEM] * 4,
        out_specs=(VMEM, VMEM),
        scratch_shapes=[
            pltpu.VMEM((width, width), F32),
            pltpu.VMEM((2, width, width), BF16),
            pltpu.VMEM((width, width), BF16),
        ],
        compiler_params=pltpu.CompilerParams(vmem_limit_bytes=BIG),
        name="solve_rows",
    )(gram, gram_other, small, small_other)
    return (update[:4].T, inverse)


def solution(mesh):
    placed = (
        P(None, ("groups", "dp")),
        P(None, ("groups", "dp")),
        P(("groups", "dp")),
        P(("groups", "dp")),
        P("groups"),
        P("groups", None),
        P("groups"),
        P("groups", None),
        P("groups"),
        P("groups", None),
        P("groups"),
    )
    return jax.shard_map(
        on_device,
        mesh=mesh,
        in_specs=placed,
        out_specs=(P(("groups", "dp"), None), P(("groups", "dp"), None)),
        check_vma=False,
    )
```

time: 444 us -> 79.4 us (0.18)
  waiting for transfers between devices: 241 us -> 0 us
  blocking collectives: 103 us -> 0 us
  Pallas kernels: 0 us -> 65.3 us
  matrix products: 59.9 us -> 0 us
  between operations: 17.1 us -> 1.31 us
  other arithmetic: 18.3 us -> 2.99 us
  local copies, waits for them, and re-layouts: 2.96 us -> 9.15 us
    all_gather x5 -> x0, waiting for transfers between devices: 240 us -> none  [on_device(): whole = lax.all_gather(iterate, 'dp', axis=0, tiled=True)]
    psum x1 -> x0, blocking collectives: 72.6 us -> none  [on_device(): lax.psum((grad_part, outer, jnp.sum(own_weights)), 'dp')]
    pallas_call x0 -> x4, Pallas kernels: none -> 65.3 us  [the longest x1 29.2 us: on_device(): pl.pallas_call(point_terms, grid=(pairs,), out_shape=(jax.ShapeDtypeStruc...]
    dot_general x16 -> x0, matrix products: 59 us -> none  [the longest x5 29.2 us: on_device(): jnp.dot(factor, whole, precision=lax.Precision.HIGHEST, preferred_element...]
    pmax x1 -> x0, blocking collectives: 30.7 us -> none  [on_device(): bound = lax.pmax(jnp.max(jnp.sum(jnp.abs(factor), 1)), 'dp')]
  transfers between devices with their start and end apart: 6 -> 0, of which waited for: 6 -> 0; matrix products, arithmetic and copies ran while one was open for 2% -> 0% of each run, Pallas kernels for 0% -> 0%
where the time goes in v1:
time: 79.4 us; the launch traced here: 78.8 us
  Pallas kernels  65.3 us (82%)
  local copies, waits for them, and re-layouts  9.15 us (12%)
  other arithmetic  2.99 us (4%)
  between operations  1.31 us (2%)
    pallas_call x1, Pallas kernels, on_device(): pl.pallas_call(point_terms, grid=(pairs,), out_shape=(jax.ShapeDtypeStruc...  29.2 us
    pallas_call x1, Pallas kernels, on_device(): pl.pallas_call(functools.partial(solve_rows, own_rows), out_shape=(jax.Sh...  17.8 us
    pallas_call x1, Pallas kernels, on_device(): pl.pallas_call(functools.partial(share_points, size), out_shape=jax.Shape...  10 us
    pallas_call x1, Pallas kernels, on_device(): pl.pallas_call(swap_sums, out_shape=(jax.ShapeDtypeStruct(gram.shape, F32...  8.32 us
    unnamed x1, local copies, waits for them, and re-layouts  3.93 us

profile of v1, /device:TPU:0, one launch (start us, length us, event | category | flops | bytes accessed | tf_op | source)
XLA Modules:
  0.0 78.8 jit_solution(8886237309585710223)
XLA Ops:
  1.3 0.7 pad_bitcast_fusion
  2.0 0.1 pad.9.clone
  2.0 0.1 pad.5.clone
  2.1 0.8 select_reduce_fusion
  2.9 0.7 copy.26.bias_ref
  3.6 0.8 maximum_select_fusion
  4.3 0.1 rev.3
  4.5 0.6 broadcast_select_fusion.own_ref
  5.1 10.0 %share_points.1.points_ref = f32[4,8,256]{2,1,0:T(8,128)} custom-call(f32[8,256]{1,0:T(8,128)} %broadcast_select_fusion.own_ref), custom_call_target="tpu_custom_call" | custom-call | tf_op jit(solution)/shard_map/share_points/pallas_call | solution.py:292
  15.1 0.8 %maximum_maximum_fusion = f32[8,1024]{1,0:T(8,128)S(1)} fusion(f32[1,1024]{1,0:T(1,128)} %bitcast.16, f32[1,1024]{1,0:T(1,128)} %bitcast.17, f32[3,1024]{1,0:T(4,128)} %param.16, f32[8]{0:T(128)S(1)} %pad.5.clone), kind=kLoop, calls=%fused_computation | loop fusion | flops 24576 | bytes 53280 | tf_op jit(solution)/shard_map/concatenate | solution.py:305
  15.9 1.3 %concatenate.14.out_ref = bf16[16,1024]{1,0:T(8,128)(2,1)} pad(bf16[4,1024]{1,0:T(4,128)(2,1)} %bitcast.15, bf16[]{:T(256)} %constant.7.clone.1), padding=0_12x0_0 | pad | bytes 40962 | tf_op jit(solution)/shard_map/concatenate | solution.py:306
  17.2 1.0 %copy.24 = f32[8,1024]{0,1:T(8,128)} copy(f32[8,1024]{1,0:T(8,128)S(1)} %maximum_maximum_fusion) | data formatting | bytes 65536 | tf_op jit(solution)/shard_map/concatenate | solution.py:305
  18.3 3.9 %copy.25 = bf16[1024,1024]{0,1:T(8,128)(2,1)} copy(bf16[1024,1024]{1,0:T(8,128)(2,1)} %param.18) | data formatting | bytes 4194304 | tf_op args[7]
  22.2 29.2 %point_terms.1 = (f32[10,256,256]{2,1,0:T(8,128)}, f32[16,1024]{1,0:T(8,128)}) custom-call(f32[4,8,256]{2,1,0:T(8,128)} %share_points.1.points_ref, f32[1024,8]{1,0:T(8,128)} %bitcast.14, bf16[1024,1024]{1,0:T(8,128)(2,1)} %bitcast.13, bf16[16,1024]{1,0:T(8,128)(2,1)} %concatenate.14.out_ref, f32[8,1]{1,0:T(8,128)} %copy.26.bias_ref), custom_call_target="tpu_custom_call" | custom-call | tf_op jit(solution)/shard_map/point_terms/pallas_call | solution.py:309
  51.4 8.3 %swap_sums.1 = (f32[10,256,256]{2,1,0:T(8,128)}, f32[16,1024]{1,0:T(8,128)}) custom-call(f32[10,256,256]{2,1,0:T(8,128)} %get-tuple-element.8.gram_ref.gram_a, f32[16,1024]{1,0:T(8,128)} %get-tuple-element.9.small_ref.small_a), custom_call_target="tpu_custom_call" | custom-call | tf_op jit(solution)/shard_map/swap_sums/pallas_call | solution.py:328
  59.7 17.8 %solve_rows.1 = (f32[64,1024]{1,0:T(8,128)}, f32[8,64]{1,0:T(8,128)}) custom-call(f32[10,256,256]{2,1,0:T(8,128)} %get-tuple-element.8.gram_ref.gram_a, f32[10,256,256]{2,1,0:T(8,128)} %get-tuple-element.10.gram_b, f32[16,1024]{1,0:T(8,128)} %get-tuple-element.9.small_ref.small_a, f32[16,1024]{1,0:T(8,128)} %get-tuple-element.11.small_b), custom_call_target="tpu_custom_call" | custom-call | tf_op jit(solution)/shard_map/solve_rows/pallas_call | solution.py:342
  77.5 1.3 %slice_bitcast_fusion = f32[64,4]{0,1:T(4,128)} fusion(f32[8,64]{1,0:T(8,128)} %get-tuple-element.12), kind=kLoop, calls=%fused_computation.5 | loop fusion | bytes 2048 | tf_op jit(solution)/shard_map/transpose | solution.py:358
  (2 shorter events, 0.0 us)

commit v2 on v1

v2 whole, which is shorter than its diff:
```python
import functools

import jax
import jax.numpy as jnp
from jax import lax
from jax.experimental import pallas as pl
from jax.experimental.pallas import tpu as pltpu
from jax.sharding import PartitionSpec as P

ITERS = 6
VISCOSITY = 0.05
DAMP_FACTOR = 1.0
DAMP_OUTPUT = 0.1

TILE = 256
MESH = pl.DeviceIdType.MESH
VMEM = pl.BlockSpec(memory_space=pltpu.VMEM)
BIG = 56 * 1024 * 1024
ROWS_DOT = (((1,), (1,)), ((), ()))
F32 = jnp.float32
BF16 = jnp.bfloat16


def share_points(
    axis_size, coords_ref, forcing_ref, bins_ref, count_ref, level_ref, w_in_ref, b_in_ref, b_mid_ref,
    mid_ref, out_ref, cols_ref, mid_out, own, held, plain, turned, send_sem, recv_sem, local_sem,
):
    half = axis_size // 2
    me = lax.axis_index("dp")
    place = me // 2
    parity = me % 2
    slots = coords_ref.shape[1]
    width = mid_ref.shape[0]
    tiles = width // TILE
    fetch = pltpu.make_async_copy(mid_ref, plain, local_sem.at[0])
    fetch.start()
    barrier = pltpu.get_barrier_semaphore()
    for hop in range(1, half):
        other = (place + hop) % half
        pl.semaphore_signal(
            barrier, inc=1, device_id={"dp": other * 2 + parity}, device_id_type=MESH
        )
    bins = bins_ref[...]
    weight = jnp.zeros((1, slots), F32)
    for level in range(level_ref.shape[1]):
        weight = jnp.where(bins == level, level_ref[0:1, level : level + 1], weight)
    at = lax.broadcasted_iota(jnp.int32, (8, slots), 0)
    every = jnp.zeros((8, slots), F32)
    for k in range(3):
        every = jnp.where(at == k, coords_ref[k : k + 1, :], every)
        every = jnp.where(at == 3 + k, forcing_ref[k : k + 1, :], every)
    every = jnp.where(at == 6, weight, every)
    slot = lax.broadcasted_iota(jnp.int32, (8, slots), 1)
    every = jnp.where(slot < count_ref[0:1, 0:1], every, F32(0.0))
    source = lax.broadcasted_iota(jnp.int32, (slots, slots), 0)
    target = lax.broadcasted_iota(jnp.int32, (slots, slots), 1)
    target = jnp.where(me >= half, slots - 1 - target, target)
    move = jnp.where(source == target, F32(1.0), F32(0.0))
    own[...] = jnp.dot(
        every, move, precision=lax.Precision.HIGHEST, preferred_element_type=F32
    )
    pl.semaphore_wait(barrier, half - 1)
    copies = []
    for hop in range(1, half):
        other = (place + hop) % half
        copy = pltpu.make_async_remote_copy(
            src_ref=own,
            dst_ref=held.at[place],
            send_sem=send_sem.at[hop],
            recv_sem=recv_sem.at[place],
            device_id={"dp": other * 2 + parity},
            device_id_type=MESH,
        )
        copy.start()
        copies.append(copy)
    held[place] = own[...]
    table = jnp.zeros((8, width), F32)
    at = lax.broadcasted_iota(jnp.int32, (8, width), 0)
    for k in range(3):
        table = jnp.where(at == k, w_in_ref[k : k + 1, :], table)
    table = jnp.where(at == 3, b_in_ref[...], table)
    table = jnp.where(at == 4, b_mid_ref[...], table)
    cols_ref[...] = table.T
    fetch.wait()
    for i in range(tiles):
        for j in range(tiles):
            turned[j * TILE : (j + 1) * TILE, i * TILE : (i + 1) * TILE] = plain[
                i * TILE : (i + 1) * TILE, j * TILE : (j + 1) * TILE
            ].T
    give = pltpu.make_async_copy(turned, mid_out, local_sem.at[1])
    give.start()
    for hop in range(1, half):
        other = (place + hop) % half
        pltpu.make_async_remote_copy(
            src_ref=own,
            dst_ref=held.at[other],
            send_sem=send_sem.at[hop],
            recv_sem=recv_sem.at[other],
            device_id={"dp": other * 2 + parity},
            device_id_type=MESH,
        ).wait_recv()
    for pair in range(half // 2):
        out_ref[pair] = held[pair] + held[pair + half // 2]
    for copy in copies:
        copy.wait_send()
    give.wait()


def point_loss(heads, height, pushes, weight):
    value, slopes, curve = heads[0], heads[1:4], heads[4]
    wall = 1.0 - height * height
    wall_slope = -2.0 * height
    vel = [wall * value[i] for i in range(3)]
    vel_slope = [[wall * slopes[k][i] for i in range(3)] for k in range(3)]
    for i in range(3):
        vel_slope[1][i] = wall_slope * value[i] + vel_slope[1][i]
    total = vel_slope[0][0] + vel_slope[1][1] + vel_slope[2][2]
    total = total * total
    for i in range(3):
        lap = -2.0 * value[i] + 2.0 * (wall_slope * slopes[1][i]) + wall * curve[i]
        convect = vel[0] * vel_slope[0][i] + vel[1] * vel_slope[1][i] + vel[2] * vel_slope[2][i]
        momentum = convect + slopes[i][3] - VISCOSITY * lap - pushes[i]
        total = total + momentum * momentum
    return 0.5 * (weight * total)


def point_terms(points_ref, cols_ref, mid_ref, out_ref, bias_ref, gram_ref, small_ref, first, jets, scaled):
    width = mid_ref.shape[0]
    pairs, _, slots = points_ref.shape
    tiles = width // TILE
    step = pl.program_id(0)

    def column(part, k):
        return cols_ref[part * TILE : (part + 1) * TILE, k : k + 1]

    def first_jet(part):
        row = [points_ref[step, k : k + 1, :] for k in range(3)]
        rows = slice(part * TILE, (part + 1) * TILE)
        w = [column(part, k) for k in range(3)]
        pre = row[0] * w[0] + row[1] * w[1] + row[2] * w[2] + column(part, 3)
        act = jnp.tanh(pre)
        slope = 1.0 - act * act
        curve_in = -2.0 * (w[0] * w[0] + w[1] * w[1] + w[2] * w[2])
        first[rows, 0:slots] = act.astype(BF16)
        for k in range(3):
            first[rows, (k + 1) * slots : (k + 2) * slots] = (slope * w[k]).astype(BF16)
        first[rows, 4 * slots : 5 * slots] = (act * slope * curve_in).astype(BF16)

    def hidden_mixed(part):
        rows = slice(part * TILE, (part + 1) * TILE)
        return jnp.dot(mid_ref[rows, :], first[...], preferred_element_type=F32)

    def hidden_jet(part, mixed):
        weight = points_ref[step, 6:7, :]
        mixed = [mixed[:, k * slots : (k + 1) * slots] for k in range(5)]
        act = jnp.tanh(mixed[0] + column(part, 4))
        slope = 1.0 - act * act
        squares = mixed[1] * mixed[1] + mixed[2] * mixed[2] + mixed[3] * mixed[3]
        jet = [act, slope * mixed[1], slope * mixed[2], slope * mixed[3]]
        jet.append(slope * (mixed[4] - 2.0 * act * squares))
        for k in range(5):
            half = jet[k].astype(BF16)
            places = slice(k * slots, (k + 1) * slots)
            jets[part * TILE : (part + 1) * TILE, places] = half
            scaled[16 + part * TILE : 16 + (part + 1) * TILE, places] = (
                half.astype(F32) * weight
            ).astype(BF16)

    def gram_rows(i):
        start = 0 if i == 0 else 16 + i * TILE
        part = lax.dot_general(
            scaled[start : 16 + (i + 1) * TILE, :],
            jets[i * TILE :, :],
            ROWS_DOT,
            preferred_element_type=F32,
        )
        if i == 0:
            small_ref[0:8, :] += part[0:8, :]
            part = part[16:, :]
        block = i * tiles - i * (i - 1) // 2
        for j in range(tiles - i):
            gram_ref[block + j] += part[:, j * TILE : (j + 1) * TILE]

    def slants():
        row = [points_ref[step - 1, k : k + 1, :] for k in range(7)]
        weight = row[6]
        heads = jnp.dot(out_ref[...], jets[...], preferred_element_type=F32)
        table = [[heads[i : i + 1, k * slots : (k + 1) * slots] for i in range(4)] for k in range(5)]
        table[0] = [table[0][i] + bias_ref[0:1, i : i + 1] for i in range(4)]
        _, pull = jax.vjp(lambda t: point_loss(t, row[1], row[3:6], weight), table)
        (slant,) = pull(jnp.ones_like(weight))
        at = lax.broadcasted_iota(jnp.int32, (16, slots), 0)
        pieces = []
        for k in range(5):
            piece = jnp.zeros((16, slots), F32)
            for i in range(4):
                piece = jnp.where(at == i, slant[k][i], piece)
            if k == 0:
                piece = jnp.where(at == 4, weight, piece)
                piece = jnp.where(at == 5, F32(1.0), piece)
            pieces.append(piece)
        cot = jnp.concatenate(pieces, 1)
        scaled[0:16, :] = cot.astype(BF16)
        small_ref[8:16, 0:8] += lax.dot_general(
            cot[0:8],
            cot[0:8],
            ROWS_DOT,
            precision=lax.Precision.HIGHEST,
            preferred_element_type=F32,
        )

    @pl.when(step == 0)
    def _():
        gram_ref[...] = jnp.zeros_like(gram_ref)
        small_ref[...] = jnp.zeros_like(small_ref)
        for part in range(tiles):
            first_jet(part)

    @pl.when((step > 0) & (step < pairs))
    def _():
        slants()
        for part in range(tiles):
            gram_rows(tiles - 1 - part)
            first_jet(part)

    @pl.when(step == pairs)
    def _():
        slants()
        for part in range(tiles):
            gram_rows(tiles - 1 - part)

    @pl.when(step < pairs)
    def _():
        mixed = hidden_mixed(0)
        for part in range(tiles):
            later = hidden_mixed(part + 1) if part + 1 < tiles else None
            hidden_jet(part, mixed)
            mixed = later


def solve_rows(
    own_rows, gram_ref, small_ref, inverse_ref, update_ref,
    gram_a, gram_b, small_b, full, high, send_sem, recv_sem, local_sem,
):
    width = full.shape[0]
    tiles = width // TILE
    blocks = gram_a.shape[0]
    me = lax.axis_index("dp")
    first_row = pl.multiple_of(me * own_rows, own_rows)
    other = me + 1 - 2 * (me % 2)
    fetch = pltpu.make_async_copy(gram_ref, gram_a, local_sem.at[0])
    fetch.start()
    barrier = pltpu.get_barrier_semaphore()
    pl.semaphore_signal(barrier, inc=1, device_id={"dp": other}, device_id_type=MESH)
    pl.semaphore_wait(barrier, 1)
    copies = []
    for at in range(blocks + 1):
        copy = pltpu.make_async_remote_copy(
            src_ref=gram_ref.at[at] if at < blocks else small_ref,
            dst_ref=gram_b.at[at] if at < blocks else small_b,
            send_sem=send_sem.at[at],
            recv_sem=recv_sem.at[at],
            device_id={"dp": other},
            device_id_type=MESH,
        )
        copies.append(copy)
    for copy in copies[-1:] + copies[:-1]:
        copy.start()
    copies[-1].wait_recv()
    small = small_ref[...] + small_b[...]
    weight_sum = small[12:13, 5:6]
    share = 1.0 / weight_sum
    fetch.wait()
    sums = [jnp.zeros((1, TILE), F32) for _ in range(tiles)]
    here = lax.broadcasted_iota(jnp.int32, (TILE, TILE), 0)
    there = lax.broadcasted_iota(jnp.int32, (TILE, TILE), 1)
    damp = jnp.where(here == there, F32(DAMP_FACTOR), F32(0.0))
    block = 0
    for i in range(tiles):
        for j in range(i, tiles):
            copies[block].wait_recv()
            piece = (gram_a[block] + gram_b[block]) * share
            block += 1
            if i == j:
                piece = piece + damp
            turned = piece.T
            rows, cols = slice(i * TILE, (i + 1) * TILE), slice(j * TILE, (j + 1) * TILE)
            full[rows, cols] = piece
            high[0, rows, cols] = piece.astype(BF16)
            sums[i] = sums[i] + jnp.sum(jnp.abs(turned), 0, keepdims=True)
            if i != j:
                full[cols, rows] = turned
                high[0, cols, rows] = turned.astype(BF16)
                sums[j] = sums[j] + jnp.sum(jnp.abs(piece), 0, keepdims=True)
    for copy in copies:
        copy.wait_send()
    largest = functools.reduce(jnp.maximum, sums)
    shrink = 1.0 / jnp.max(largest, 1, keepdims=True)
    mine = full[pl.ds(first_row, own_rows), :]
    at_row = lax.broadcasted_iota(jnp.int32, mine.shape, 0) + first_row
    at_col = lax.broadcasted_iota(jnp.int32, mine.shape, 1)
    iterate = jnp.where(at_row == at_col, F32(2.0), F32(0.0)) - mine * shrink

    def split(value):
        upper = value.astype(BF16)
        return upper, (value - upper.astype(F32)).astype(BF16)

    def times(value, at):
        both = jnp.concatenate(split(value), 0)
        both = jnp.dot(both, high[at, 0:width, :], preferred_element_type=F32)
        return both[:own_rows] + both[own_rows:]

    at = 0
    for turn in range(ITERS - 2):
        if turn > 0:
            upper, lower = split(iterate)
            high[at, width : width + own_rows, :] = upper
            high[at, width + own_rows : width + 2 * own_rows, :] = lower
        reach = width + 2 * own_rows if turn > 0 else width
        products = []
        for j in range(tiles):
            cols = slice(j * TILE, (j + 1) * TILE)
            square = jnp.dot(
                high[at, 0:reach, :], high[at, 0:width, cols], preferred_element_type=F32
            )
            if turn == 0:
                later = shrink * (2.0 * full[:, cols] - shrink * square)
            else:
                later = 2.0 * full[:, cols] - square[0:width]
                products.append(
                    square[width : width + own_rows] + square[width + own_rows :]
                )
            full[:, cols] = later
            high[1 - at, 0:width, cols] = later.astype(BF16)
        if turn > 0:
            iterate = 2.0 * iterate - jnp.concatenate(products, 1)
        at = 1 - at
    iterate = 2.0 * iterate - times(iterate, at)
    turned = iterate - times(iterate, at)
    turned = turned - times(turned, at)
    iterate = (iterate + turned) * shrink
    inverse_ref[...] = iterate
    merged = lax.dot_general(
        small[0:8, :] / weight_sum,
        iterate,
        ROWS_DOT,
        precision=lax.Precision.HIGHEST,
        preferred_element_type=F32,
    )
    outer = [[small[8 + i : 9 + i, j : j + 1] for j in range(4)] for i in range(4)]
    trace = outer[0][0] + outer[1][1] + outer[2][2] + outer[3][3]
    lower = [[None] * 4 for _ in range(4)]
    for i in range(4):
        for j in range(i + 1):
            entry = 4.0 * outer[i][j] / trace
            if i == j:
                entry = entry + DAMP_OUTPUT
            for k in range(j):
                entry = entry - lower[i][k] * lower[j][k]
            lower[i][j] = jnp.sqrt(entry) if i == j else entry / lower[j][j]
    solved = [merged[i : i + 1, :] for i in range(4)]
    for i in range(4):
        for k in range(i):
            solved[i] = solved[i] - lower[i][k] * solved[k]
        solved[i] = solved[i] / lower[i][i]
    for i in reversed(range(4)):
        for k in range(i + 1, 4):
            solved[i] = solved[i] - lower[k][i] * solved[k]
        solved[i] = solved[i] / lower[i][i]
    at = lax.broadcasted_iota(jnp.int32, (4, own_rows), 0)
    update = jnp.zeros((4, own_rows), F32)
    for i in range(4):
        update = jnp.where(at == i, solved[i], update)
    update_ref[...] = update


def on_device(coords, forcing, bins, counts, bin_weight, w_in, b_in, w_mid, b_mid, w_out, b_out):
    slots = coords.shape[1]
    width = w_mid.shape[0]
    size = lax.axis_size("dp")
    half = size // 2
    pairs = half // 2
    tiles = width // TILE
    blocks = tiles * (tiles + 1) // 2
    own_rows = width // size
    points, cols, mid = pl.pallas_call(
        functools.partial(share_points, size),
        out_shape=(
            jax.ShapeDtypeStruct((pairs, 8, slots), F32),
            jax.ShapeDtypeStruct((width, 8), F32),
            jax.ShapeDtypeStruct((width, width), BF16),
        ),
        in_specs=[VMEM] * 8 + [pl.BlockSpec(memory_space=pl.ANY)],
        out_specs=(VMEM, VMEM, pl.BlockSpec(memory_space=pl.ANY)),
        scratch_shapes=[
            pltpu.VMEM((8, slots), F32),
            pltpu.VMEM((half, 8, slots), F32),
            pltpu.VMEM((width, width), BF16),
            pltpu.VMEM((width, width), BF16),
            pltpu.SemaphoreType.DMA((half,)),
            pltpu.SemaphoreType.DMA((half,)),
            pltpu.SemaphoreType.DMA((2,)),
        ],
        compiler_params=pltpu.CompilerParams(
            collective_id=0, has_side_effects=True, vmem_limit_bytes=BIG
        ),
        name="share_points",
    )(
        coords, forcing, bins[None], counts[None], bin_weight[None], w_in, b_in[None], b_mid[None],
        w_mid,
    )
    fixed = lambda *shape: pl.BlockSpec(shape, lambda i: (0,) * len(shape))
    gram, small = pl.pallas_call(
        point_terms,
        grid=(pairs + 1,),
        out_shape=(
            jax.ShapeDtypeStruct((blocks, TILE, TILE), F32),
            jax.ShapeDtypeStruct((16, width), F32),
        ),
        in_specs=[
            fixed(pairs, 8, slots),
            fixed(width, 8),
            fixed(width, width),
            fixed(4, width),
            fixed(1, 4),
        ],
        out_specs=(fixed(blocks, TILE, TILE), fixed(16, width)),
        scratch_shapes=[
            pltpu.VMEM((width, 5 * slots), BF16),
            pltpu.VMEM((width, 5 * slots), BF16),
            pltpu.VMEM((width + 16, 5 * slots), BF16),
        ],
        compiler_params=pltpu.CompilerParams(vmem_limit_bytes=BIG),
        name="point_terms",
    )(points, cols, mid, w_out.T, b_out[None])
    inverse, update = pl.pallas_call(
        functools.partial(solve_rows, own_rows),
        out_shape=(
            jax.ShapeDtypeStruct((own_rows, width), F32),
            jax.ShapeDtypeStruct((4, own_rows), F32),
        ),
        in_specs=[pl.BlockSpec(memory_space=pl.ANY), VMEM],
        out_specs=(VMEM, VMEM),
        scratch_shapes=[
            pltpu.VMEM((blocks, TILE, TILE), F32),
            pltpu.VMEM((blocks, TILE, TILE), F32),
            pltpu.VMEM((16, width), F32),
            pltpu.VMEM((width, width), F32),
            pltpu.VMEM((2, width + 2 * own_rows, width), BF16),
            pltpu.SemaphoreType.DMA((blocks + 1,)),
            pltpu.SemaphoreType.DMA((blocks + 1,)),
            pltpu.SemaphoreType.DMA((1,)),
        ],
        compiler_params=pltpu.CompilerParams(
            collective_id=1, has_side_effects=True, vmem_limit_bytes=BIG
        ),
        name="solve_rows",
    )(gram, small)
    return (update.T, inverse)


def solution(mesh):
    placed = (
        P(None, ("groups", "dp")),
        P(None, ("groups", "dp")),
        P(("groups", "dp")),
        P(("groups", "dp")),
        P("groups"),
        P("groups", None),
        P("groups"),
        P("groups", None),
        P("groups"),
        P("groups", None),
        P("groups"),
    )
    return jax.shard_map(
        on_device,
        mesh=mesh,
        in_specs=placed,
        out_specs=(P(("groups", "dp"), None), P(("groups", "dp"), None)),
        check_vma=False,
    )
```

time: 79.4 us -> 61.1 us (0.77)
  Pallas kernels: 65.3 us -> 56.6 us
  local copies, waits for them, and re-layouts: 9.15 us -> 2.92 us
  other arithmetic: 2.99 us -> 0 us
    pallas_call x3 -> x2, Pallas kernels: 47.6 us -> 38.2 us  [the longest x1 27.9 us: on_device(): pl.pallas_call(point_terms, grid=(pairs + 1,), out_shape=(jax.ShapeDtypeS...]
    concatenate x4 -> x0, local copies, waits for them, and re-layouts: 2.48 us -> none  [the longest x1 1.32 us: on_device(): out_rows = jnp.concatenate([w_out.T, jnp.zeros((12, width), BF16)], 0)]
    select_n x2 -> x0, other arithmetic: 1.38 us -> none  [the longest x1 0.77 us: packed_points(): every = jnp.where(live[None, :], every, F32(0.0))]
    broadcast_in_dim x3 -> x0, local copies, waits for them, and re-layouts: 1.33 us -> none  [the longest x2 1.33 us: on_device(): bias = jnp.concatenate([b_out, jnp.zeros((4,), F32)])[:, None]]
    transpose x1 -> x0, local copies, waits for them, and re-layouts: 1.26 us -> none  [on_device(): return (update[:4].T, inverse)]
    unnamed x1 -> x2, local copies, waits for them, and re-layouts: 3.93 us -> 2.92 us
    concatenate x1 -> x0, other arithmetic: 0.82 us -> none  [on_device(): jnp.concatenate([w_in, b_in[None], b_mid[None], jnp.zeros((3, width), F32...]
where the time goes in v2:
time: 61.1 us; the launch traced here: 60.8 us
  Pallas kernels  56.6 us (93%)
  local copies, waits for them, and re-layouts  2.92 us (5%)
  between operations  1.3 us (2%)
    pallas_call x1, Pallas kernels, on_device(): pl.pallas_call(point_terms, grid=(pairs + 1,), out_shape=(jax.ShapeDtypeS...  27.9 us
    pallas_call x1, Pallas kernels, on_device(): pl.pallas_call(functools.partial(solve_rows, own_rows), out_shape=(jax.Sh...  18.4 us
    pallas_call x1, Pallas kernels, on_device(): pl.pallas_call(functools.partial(share_points, size), out_shape=(jax.Shap...  10.4 us
    unnamed x2, local copies, waits for them, and re-layouts  2.92 us

profile of v2, /device:TPU:0, one launch (start us, length us, event | category | flops | bytes accessed | tf_op | source)
XLA Modules:
  0.0 60.8 jit_solution(2132034686261186938)
XLA Ops:
  1.3 10.4 %share_points.1 = (f32[4,8,256]{2,1,0:T(8,128)}, f32[1024,8]{1,0:T(8,128)}, bf16[1024,1024]{1,0:T(8,128)(2,1)}) custom-call(f32[3,256]{1,0:T(4,128)} %coords_ref.1, f32[3,256]{1,0:T(4,128)} %forcing_ref.1, s32[1,256]{1,0:T(1,128)} %bitcast.13, s32[1,1]{1,0:T(1,128)} %bitcast.8.count_ref, f32[1,16]{1,0:T(1,128)} %bitcast.14, f32[3,1024]{1,0:T(4,128)} %w_in_ref.1, ...), custom_call_target="tpu_custom_call" | custom-call | tf_op jit(solution)/shard_map/share_points/pallas_call | solution.py:386
  11.7 27.9 %point_terms.1 = (f32[10,256,256]{2,1,0:T(8,128)}, f32[16,1024]{1,0:T(8,128)}) custom-call(f32[4,8,256]{2,1,0:T(8,128)} %get-tuple-element.9.points_ref, f32[1024,8]{1,0:T(8,128)} %get-tuple-element.10.cols_ref, bf16[1024,1024]{1,0:T(8,128)(2,1)} %get-tuple-element.11.mid_ref, bf16[4,1024]{1,0:T(4,128)(2,1)} %bitcast.9, f32[1,4]{1,0:T(1,128)} %bitcast.15), custom_call_target="tpu_custom_call" | custom-call | tf_op jit(solution)/shard_map/point_terms/pallas_call | solution.py:413
  39.5 18.4 %solve_rows.1 = (f32[64,1024]{1,0:T(8,128)}, f32[4,64]{1,0:T(4,128)}) custom-call(f32[10,256,256]{2,1,0:T(8,128)} %get-tuple-element.12.gram_ref, f32[16,1024]{1,0:T(8,128)} %get-tuple-element.13.small_ref), custom_call_target="tpu_custom_call" | custom-call | tf_op jit(solution)/shard_map/solve_rows/pallas_call | solution.py:436
  57.9 1.2 %copy.16 = f32[64,4]{0,1:T(4,128)} copy(f32[64,4]{0,1:T(4,128)} %bitcast.12) | data formatting | bytes 2048
  59.1 1.7 %copy.17 = f32[64,1024]{1,0:T(8,128)} copy(f32[64,1024]{1,0:T(8,128)} %get-tuple-element.19) | data formatting | bytes 524288

commit v3 on v2

--- a/solution.py
+++ b/solution.py
@@ -124,11 +124,14 @@
     return 0.5 * (weight * total)
 
 
-def point_terms(points_ref, cols_ref, mid_ref, out_ref, bias_ref, gram_ref, small_ref, first, jets, scaled):
+def point_terms(points_ref, cols_ref, mid_ref, out_ref, bias_ref, gram_ref, small_ref, first, jets, scaled, gram_b, small_b, send_sem, recv_sem):
     width = mid_ref.shape[0]
     pairs, _, slots = points_ref.shape
     tiles = width // TILE
     step = pl.program_id(0)
+    me = lax.axis_index("dp")
+    other = me + 1 - 2 * (me % 2)
+    barrier = pltpu.get_barrier_semaphore()
 
     def column(part, k):
         return cols_ref[part * TILE : (part + 1) * TILE, k : k + 1]
@@ -146,25 +149,37 @@
             first[rows, (k + 1) * slots : (k + 2) * slots] = (slope * w[k]).astype(BF16)
         first[rows, 4 * slots : 5 * slots] = (act * slope * curve_in).astype(BF16)
 
-    def hidden_mixed(part):
+    def hidden_mixed(part, k):
         rows = slice(part * TILE, (part + 1) * TILE)
-        return jnp.dot(mid_ref[rows, :], first[...], preferred_element_type=F32)
-
-    def hidden_jet(part, mixed):
+        return jnp.dot(
+            mid_ref[rows, :], first[:, k * slots : (k + 1) * slots], preferred_element_type=F32
+        )
+
+    def keep_jet(part, k, jet):
         weight = points_ref[step, 6:7, :]
-        mixed = [mixed[:, k * slots : (k + 1) * slots] for k in range(5)]
-        act = jnp.tanh(mixed[0] + column(part, 4))
-        slope = 1.0 - act * act
-        squares = mixed[1] * mixed[1] + mixed[2] * mixed[2] + mixed[3] * mixed[3]
-        jet = [act, slope * mixed[1], slope * mixed[2], slope * mixed[3]]
-        jet.append(slope * (mixed[4] - 2.0 * act * squares))
-        for k in range(5):
-            half = jet[k].astype(BF16)
-            places = slice(k * slots, (k + 1) * slots)
-            jets[part * TILE : (part + 1) * TILE, places] = half
-            scaled[16 + part * TILE : 16 + (part + 1) * TILE, places] = (
-                half.astype(F32) * weight
-            ).astype(BF16)
+        places = slice(k * slots, (k + 1) * slots)
+        jets[part * TILE : (part + 1) * TILE, places] = jet.astype(BF16)
+        scaled[16 + part * TILE : 16 + (part + 1) * TILE, places] = (jet * weight).astype(BF16)
+
+    def hidden_jets():
+        mixed = [hidden_mixed(0, k) for k in range(5)]
+        for part in range(tiles):
+            later = []
+            for k in range(5):
+                if part + 1 < tiles:
+                    later.append(hidden_mixed(part + 1, k))
+                if k == 0:
+                    act = jnp.tanh(mixed[0] + column(part, 4))
+                    slope = 1.0 - act * act
+                    jet = act
+                elif k < 4:
+                    square = mixed[k] * mixed[k]
+                    squares = square if k == 1 else squares + square
+                    jet = slope * mixed[k]
+                else:
+                    jet = slope * (mixed[4] - 2.0 * act * squares)
+                keep_jet(part, k, jet)
+            mixed = later
 
     def gram_rows(i):
         start = 0 if i == 0 else 16 + i * TILE
@@ -211,10 +226,13 @@
 
     @pl.when(step == 0)
     def _():
+        pl.semaphore_signal(barrier, inc=1, device_id={"dp": other}, device_id_type=MESH)
         gram_ref[...] = jnp.zeros_like(gram_ref)
         small_ref[...] = jnp.zeros_like(small_ref)
         for part in range(tiles):
             first_jet(part)
+
+        hidden_jets()
 
     @pl.when((step > 0) & (step < pairs))
     def _():
@@ -222,55 +240,44 @@
         for part in range(tiles):
             gram_rows(tiles - 1 - part)
             first_jet(part)
+        hidden_jets()
 
     @pl.when(step == pairs)
     def _():
         slants()
-        for part in range(tiles):
-            gram_rows(tiles - 1 - part)
-
-    @pl.when(step < pairs)
-    def _():
-        mixed = hidden_mixed(0)
-        for part in range(tiles):
-            later = hidden_mixed(part + 1) if part + 1 < tiles else None
-            hidden_jet(part, mixed)
-            mixed = later
-
-
-def solve_rows(
-    own_rows, gram_ref, small_ref, inverse_ref, update_ref,
-    gram_a, gram_b, small_b, full, high, send_sem, recv_sem, local_sem,
-):
+        copies = []
+
+        def send(at, source, target):
+            copy = pltpu.make_async_remote_copy(
+                src_ref=source,
+                dst_ref=target,
+                send_sem=send_sem.at[at],
+                recv_sem=recv_sem.at[at],
+                device_id={"dp": other},
+                device_id_type=MESH,
+            )
+            copy.start()
+            copies.append((copy, source, target))
+
+        pl.semaphore_wait(barrier, 1)
+        for i in reversed(range(tiles)):
+            gram_rows(i)
+            block = i * tiles - i * (i - 1) // 2
+            for j in range(tiles - i):
+                send(block + j, gram_ref.at[block + j], gram_b.at[block + j])
+        send(gram_ref.shape[0], small_ref, small_b)
+        for copy, source, target in copies:
+            copy.wait()
+            source[...] += target[...]
+
+
+def solve_rows(own_rows, gram_ref, small_ref, inverse_ref, update_ref, full, high):
     width = full.shape[0]
     tiles = width // TILE
-    blocks = gram_a.shape[0]
-    me = lax.axis_index("dp")
-    first_row = pl.multiple_of(me * own_rows, own_rows)
-    other = me + 1 - 2 * (me % 2)
-    fetch = pltpu.make_async_copy(gram_ref, gram_a, local_sem.at[0])
-    fetch.start()
-    barrier = pltpu.get_barrier_semaphore()
-    pl.semaphore_signal(barrier, inc=1, device_id={"dp": other}, device_id_type=MESH)
-    pl.semaphore_wait(barrier, 1)
-    copies = []
-    for at in range(blocks + 1):
-        copy = pltpu.make_async_remote_copy(
-            src_ref=gram_ref.at[at] if at < blocks else small_ref,
-            dst_ref=gram_b.at[at] if at < blocks else small_b,
-            send_sem=send_sem.at[at],
-            recv_sem=recv_sem.at[at],
-            device_id={"dp": other},
-            device_id_type=MESH,
-        )
-        copies.append(copy)
-    for copy in copies[-1:] + copies[:-1]:
-        copy.start()
-    copies[-1].wait_recv()
-    small = small_ref[...] + small_b[...]
+    first_row = pl.multiple_of(lax.axis_index("dp") * own_rows, own_rows)
+    small = small_ref[...]
     weight_sum = small[12:13, 5:6]
     share = 1.0 / weight_sum
-    fetch.wait()
     sums = [jnp.zeros((1, TILE), F32) for _ in range(tiles)]
     here = lax.broadcasted_iota(jnp.int32, (TILE, TILE), 0)
     there = lax.broadcasted_iota(jnp.int32, (TILE, TILE), 1)
@@ -278,8 +285,7 @@
     block = 0
     for i in range(tiles):
         for j in range(i, tiles):
-            copies[block].wait_recv()
-            piece = (gram_a[block] + gram_b[block]) * share
+            piece = gram_ref[block] * share
             block += 1
             if i == j:
                 piece = piece + damp
@@ -292,8 +298,6 @@
                 full[cols, rows] = turned
                 high[0, cols, rows] = turned.astype(BF16)
                 sums[j] = sums[j] + jnp.sum(jnp.abs(piece), 0, keepdims=True)
-    for copy in copies:
-        copy.wait_send()
     largest = functools.reduce(jnp.maximum, sums)
     shrink = 1.0 / jnp.max(largest, 1, keepdims=True)
     mine = full[pl.ds(first_row, own_rows), :]
@@ -429,8 +433,14 @@
             pltpu.VMEM((width, 5 * slots), BF16),
             pltpu.VMEM((width, 5 * slots), BF16),
             pltpu.VMEM((width + 16, 5 * slots), BF16),
+            pltpu.VMEM((blocks, TILE, TILE), F32),
+            pltpu.VMEM((16, width), F32),
+            pltpu.SemaphoreType.DMA((blocks + 1,)),
+            pltpu.SemaphoreType.DMA((blocks + 1,)),
         ],
-        compiler_params=pltpu.CompilerParams(vmem_limit_bytes=BIG),
+        compiler_params=pltpu.CompilerParams(
+            collective_id=1, has_side_effects=True, vmem_limit_bytes=BIG
+        ),
         name="point_terms",
     )(points, cols, mid, w_out.T, b_out[None])
     inverse, update = pl.pallas_call(
@@ -439,21 +449,13 @@
             jax.ShapeDtypeStruct((own_rows, width), F32),
             jax.ShapeDtypeStruct((4, own_rows), F32),
         ),
-        in_specs=[pl.BlockSpec(memory_space=pl.ANY), VMEM],
+        in_specs=[VMEM, VMEM],
         out_specs=(VMEM, VMEM),
         scratch_shapes=[
-            pltpu.VMEM((blocks, TILE, TILE), F32),
-            pltpu.VMEM((blocks, TILE, TILE), F32),
-            pltpu.VMEM((16, width), F32),
             pltpu.VMEM((width, width), F32),
             pltpu.VMEM((2, width + 2 * own_rows, width), BF16),
-            pltpu.SemaphoreType.DMA((blocks + 1,)),
-            pltpu.SemaphoreType.DMA((blocks + 1,)),
-            pltpu.SemaphoreType.DMA((1,)),
         ],
-        compiler_params=pltpu.CompilerParams(
-            collective_id=1, has_side_effects=True, vmem_limit_bytes=BIG
-        ),
+        compiler_params=pltpu.CompilerParams(vmem_limit_bytes=BIG),
         name="solve_rows",
     )(gram, small)
     return (update.T, inverse)

time: 61.1 us -> 57.6 us (0.943)
  local copies, waits for them, and re-layouts: 2.92 us -> 0 us
    pallas_call x1, Pallas kernels: 18.4 us -> 14 us  [on_device(): pl.pallas_call(functools.partial(solve_rows, own_rows), out_shape=(jax.Sh...]
    pallas_call x1, Pallas kernels: 27.9 us -> 31.7 us  [on_device(): pl.pallas_call(point_terms, grid=(pairs + 1,), out_shape=(jax.ShapeDtypeS...]
    unnamed x2 -> x0, local copies, waits for them, and re-layouts: 2.92 us -> none
where the time goes in v3:
time: 57.6 us; the launch traced here: 57.3 us
  Pallas kernels  56 us (97%)
  between operations  1.29 us (2%)
    pallas_call x1, Pallas kernels, on_device(): pl.pallas_call(point_terms, grid=(pairs + 1,), out_shape=(jax.ShapeDtypeS...  31.7 us
    pallas_call x1, Pallas kernels, on_device(): pl.pallas_call(functools.partial(solve_rows, own_rows), out_shape=(jax.Sh...  14 us
    pallas_call x1, Pallas kernels, on_device(): pl.pallas_call(functools.partial(share_points, size), out_shape=(jax.Shap...  10.4 us

profile of v3, /device:TPU:0, one launch (start us, length us, event | category | flops | bytes accessed | tf_op | source)
XLA Modules:
  0.0 57.3 jit_solution(11289655829727052078)
XLA Ops:
  1.3 10.4 %share_points.1 = (f32[4,8,256]{2,1,0:T(8,128)}, f32[1024,8]{1,0:T(8,128)}, bf16[1024,1024]{1,0:T(8,128)(2,1)}) custom-call(f32[3,256]{1,0:T(4,128)} %coords_ref.1, f32[3,256]{1,0:T(4,128)} %forcing_ref.1, s32[1,256]{1,0:T(1,128)} %bitcast.12, s32[1,1]{1,0:T(1,128)} %bitcast.8.count_ref, f32[1,16]{1,0:T(1,128)} %bitcast.13, f32[3,1024]{1,0:T(4,128)} %w_in_ref.1, ...), custom_call_target="tpu_custom_call" | custom-call | tf_op jit(solution)/shard_map/share_points/pallas_call | solution.py:390
  11.7 31.7 %point_terms.1 = (f32[10,256,256]{2,1,0:T(8,128)}, f32[16,1024]{1,0:T(8,128)}) custom-call(f32[4,8,256]{2,1,0:T(8,128)} %get-tuple-element.9.points_ref, f32[1024,8]{1,0:T(8,128)} %get-tuple-element.10.cols_ref, bf16[1024,1024]{1,0:T(8,128)(2,1)} %get-tuple-element.11.mid_ref, bf16[4,1024]{1,0:T(4,128)(2,1)} %bitcast.9, f32[1,4]{1,0:T(1,128)} %bitcast.14), custom_call_target="tpu_custom_call" | custom-call | tf_op jit(solution)/shard_map/point_terms/pallas_call | solution.py:417
  43.3 14.0 %solve_rows.1 = (f32[64,1024]{1,0:T(8,128)}, f32[4,64]{1,0:T(4,128)}) custom-call(f32[10,256,256]{2,1,0:T(8,128)} %get-tuple-element.12.gram_ref, f32[16,1024]{1,0:T(8,128)} %get-tuple-element.13.small_ref), custom_call_target="tpu_custom_call" | custom-call | tf_op jit(solution)/shard_map/solve_rows/pallas_call | solution.py:446

commit v4 on v3

--- a/solution.py
+++ b/solution.py
@@ -274,6 +274,7 @@
 def solve_rows(own_rows, gram_ref, small_ref, inverse_ref, update_ref, full, high):
     width = full.shape[0]
     tiles = width // TILE
+    lead = 2 * own_rows
     first_row = pl.multiple_of(lax.axis_index("dp") * own_rows, own_rows)
     small = small_ref[...]
     weight_sum = small[12:13, 5:6]
@@ -292,11 +293,11 @@
             turned = piece.T
             rows, cols = slice(i * TILE, (i + 1) * TILE), slice(j * TILE, (j + 1) * TILE)
             full[rows, cols] = piece
-            high[0, rows, cols] = piece.astype(BF16)
+            high[0, lead + rows.start : lead + rows.stop, cols] = piece.astype(BF16)
             sums[i] = sums[i] + jnp.sum(jnp.abs(turned), 0, keepdims=True)
             if i != j:
                 full[cols, rows] = turned
-                high[0, cols, rows] = turned.astype(BF16)
+                high[0, lead + cols.start : lead + cols.stop, rows] = turned.astype(BF16)
                 sums[j] = sums[j] + jnp.sum(jnp.abs(piece), 0, keepdims=True)
     largest = functools.reduce(jnp.maximum, sums)
     shrink = 1.0 / jnp.max(largest, 1, keepdims=True)
@@ -311,31 +312,35 @@
 
     def times(value, at):
         both = jnp.concatenate(split(value), 0)
-        both = jnp.dot(both, high[at, 0:width, :], preferred_element_type=F32)
+        both = jnp.dot(both, high[at, lead:, :], preferred_element_type=F32)
         return both[:own_rows] + both[own_rows:]
 
     at = 0
     for turn in range(ITERS - 2):
         if turn > 0:
             upper, lower = split(iterate)
-            high[at, width : width + own_rows, :] = upper
-            high[at, width + own_rows : width + 2 * own_rows, :] = lower
-        reach = width + 2 * own_rows if turn > 0 else width
-        products = []
-        for j in range(tiles):
+            high[at, 0:own_rows, :] = upper
+            high[at, own_rows:lead, :] = lower
+        start = 0 if turn > 0 else lead
+        products = [None] * tiles
+        for j in reversed(range(tiles)):
             cols = slice(j * TILE, (j + 1) * TILE)
+            reach = (j + 1) * TILE
             square = jnp.dot(
-                high[at, 0:reach, :], high[at, 0:width, cols], preferred_element_type=F32
+                high[at, start : lead + reach, :], high[at, lead:, cols], preferred_element_type=F32
             )
             if turn == 0:
-                later = shrink * (2.0 * full[:, cols] - shrink * square)
+                later = shrink * (2.0 * full[0:reach, cols] - shrink * square)
             else:
-                later = 2.0 * full[:, cols] - square[0:width]
-                products.append(
-                    square[width : width + own_rows] + square[width + own_rows :]
-                )
-            full[:, cols] = later
-            high[1 - at, 0:width, cols] = later.astype(BF16)
+                products[j] = square[0:own_rows] + square[own_rows:lead]
+                later = 2.0 * full[0:reach, cols] - square[lead:]
+            full[0:reach, cols] = later
+            half = later.astype(BF16)
+            high[1 - at, lead : lead + reach, cols] = half
+            for i in range(j):
+                high[1 - at, lead + cols.start : lead + cols.stop, i * TILE : (i + 1) * TILE] = half[
+                    i * TILE : (i + 1) * TILE
+                ].T
         if turn > 0:
             iterate = 2.0 * iterate - jnp.concatenate(products, 1)
         at = 1 - at

time: 57.6 us -> 54.5 us (0.946)
  Pallas kernels: 56 us -> 53 us
    pallas_call x1, Pallas kernels: 14 us -> 10.9 us  [on_device(): pl.pallas_call(functools.partial(solve_rows, own_rows), out_shape=(jax.Sh...]
where the time goes in v4:
time: 54.5 us; the launch traced here: 54.3 us
  Pallas kernels  53 us (97%)
  between operations  1.29 us (2%)
    pallas_call x1, Pallas kernels, on_device(): pl.pallas_call(point_terms, grid=(pairs + 1,), out_shape=(jax.ShapeDtypeS...  31.7 us
    pallas_call x1, Pallas kernels, on_device(): pl.pallas_call(functools.partial(solve_rows, own_rows), out_shape=(jax.Sh...  10.9 us
    pallas_call x1, Pallas kernels, on_device(): pl.pallas_call(functools.partial(share_points, size), out_shape=(jax.Shap...  10.4 us

profile of v4, /device:TPU:0, one launch (start us, length us, event | category | flops | bytes accessed | tf_op | source)
XLA Modules:
  0.0 54.3 jit_solution(12878504708835374855)
XLA Ops:
  1.3 10.4 %share_points.1 = (f32[4,8,256]{2,1,0:T(8,128)}, f32[1024,8]{1,0:T(8,128)}, bf16[1024,1024]{1,0:T(8,128)(2,1)}) custom-call(f32[3,256]{1,0:T(4,128)} %coords_ref.1, f32[3,256]{1,0:T(4,128)} %forcing_ref.1, s32[1,256]{1,0:T(1,128)} %bitcast.12, s32[1,1]{1,0:T(1,128)} %bitcast.8.count_ref, f32[1,16]{1,0:T(1,128)} %bitcast.13, f32[3,1024]{1,0:T(4,128)} %w_in_ref.1, ...), custom_call_target="tpu_custom_call" | custom-call | tf_op jit(solution)/shard_map/share_points/pallas_call | solution.py:395
  11.7 31.7 %point_terms.1 = (f32[10,256,256]{2,1,0:T(8,128)}, f32[16,1024]{1,0:T(8,128)}) custom-call(f32[4,8,256]{2,1,0:T(8,128)} %get-tuple-element.9.points_ref, f32[1024,8]{1,0:T(8,128)} %get-tuple-element.10.cols_ref, bf16[1024,1024]{1,0:T(8,128)(2,1)} %get-tuple-element.11.mid_ref, bf16[4,1024]{1,0:T(4,128)(2,1)} %bitcast.9, f32[1,4]{1,0:T(1,128)} %bitcast.14), custom_call_target="tpu_custom_call" | custom-call | tf_op jit(solution)/shard_map/point_terms/pallas_call | solution.py:422
  43.3 10.9 %solve_rows.1 = (f32[64,1024]{1,0:T(8,128)}, f32[4,64]{1,0:T(4,128)}) custom-call(f32[10,256,256]{2,1,0:T(8,128)} %get-tuple-element.12.gram_ref, f32[16,1024]{1,0:T(8,128)} %get-tuple-element.13.small_ref), custom_call_target="tpu_custom_call" | custom-call | tf_op jit(solution)/shard_map/solve_rows/pallas_call | solution.py:451

commit v5 on v4

--- a/solution.py
+++ b/solution.py
@@ -244,7 +244,6 @@
 
     @pl.when(step == pairs)
     def _():
-        slants()
         copies = []
 
         def send(at, source, target):
@@ -261,6 +260,8 @@
 
         pl.semaphore_wait(barrier, 1)
         for i in reversed(range(tiles)):
+            if i == 0:
+                slants()
             gram_rows(i)
             block = i * tiles - i * (i - 1) // 2
             for j in range(tiles - i):

time: 54.5 us -> 54.2 us (level)
  no operation moved by 1% of the time
where the time goes in v5:
time: 54.2 us; the launch traced here: 54 us
  Pallas kernels  52.7 us (97%)
  between operations  1.29 us (2%)
    pallas_call x1, Pallas kernels, on_device(): pl.pallas_call(point_terms, grid=(pairs + 1,), out_shape=(jax.ShapeDtypeS...  31.4 us
    pallas_call x1, Pallas kernels, on_device(): pl.pallas_call(functools.partial(solve_rows, own_rows), out_shape=(jax.Sh...  10.9 us
    pallas_call x1, Pallas kernels, on_device(): pl.pallas_call(functools.partial(share_points, size), out_shape=(jax.Shap...  10.4 us

profile of v5, /device:TPU:0, one launch (start us, length us, event | category | flops | bytes accessed | tf_op | source)
XLA Modules:
  0.0 54.0 jit_solution(9978266511933460586)
XLA Ops:
  1.3 10.4 %share_points.1 = (f32[4,8,256]{2,1,0:T(8,128)}, f32[1024,8]{1,0:T(8,128)}, bf16[1024,1024]{1,0:T(8,128)(2,1)}) custom-call(f32[3,256]{1,0:T(4,128)} %coords_ref.1, f32[3,256]{1,0:T(4,128)} %forcing_ref.1, s32[1,256]{1,0:T(1,128)} %bitcast.12, s32[1,1]{1,0:T(1,128)} %bitcast.8.count_ref, f32[1,16]{1,0:T(1,128)} %bitcast.13, f32[3,1024]{1,0:T(4,128)} %w_in_ref.1, ...), custom_call_target="tpu_custom_call" | custom-call | tf_op jit(solution)/shard_map/share_points/pallas_call | solution.py:396
  11.7 31.4 %point_terms.1 = (f32[10,256,256]{2,1,0:T(8,128)}, f32[16,1024]{1,0:T(8,128)}) custom-call(f32[4,8,256]{2,1,0:T(8,128)} %get-tuple-element.9.points_ref, f32[1024,8]{1,0:T(8,128)} %get-tuple-element.10.cols_ref, bf16[1024,1024]{1,0:T(8,128)(2,1)} %get-tuple-element.11.mid_ref, bf16[4,1024]{1,0:T(4,128)(2,1)} %bitcast.9, f32[1,4]{1,0:T(1,128)} %bitcast.14), custom_call_target="tpu_custom_call" | custom-call | tf_op jit(solution)/shard_map/point_terms/pallas_call | solution.py:423
  43.0 10.9 %solve_rows.1 = (f32[64,1024]{1,0:T(8,128)}, f32[4,64]{1,0:T(4,128)}) custom-call(f32[10,256,256]{2,1,0:T(8,128)} %get-tuple-element.12.gram_ref, f32[16,1024]{1,0:T(8,128)} %get-tuple-element.13.small_ref), custom_call_target="tpu_custom_call" | custom-call | tf_op jit(solution)/shard_map/solve_rows/pallas_call | solution.py:452
